TPU v7x, 128 devices: a whole 4x4x4 slice. The times are simulated.
128 devices in a mesh: ctx: 16 (over x, z_lo, core), dp: 8 (over z_hi, y).
Axes of the slice: x: 4, y: 4, z: 4 (z_hi: 2, z_lo: 2; z = z_hi * 2 + z_lo), core: 2. Of those that a mesh axis runs over, the one named last changes fastest.
Arguments:
- tokens: bfloat16 [1024, 4096], P(('ctx', 'dp')), may hold values from -6 to 6
- cotangent: bfloat16 [1024, 4096], P(('ctx', 'dp')), may hold values from -6 to 6
- expert_ids: int32 [1024, 8], P(('ctx', 'dp')), may hold values from 0 to 63, as said below
- gates: float32 [1024, 8], P(('ctx', 'dp')), may hold values from 0.03 to 0.5
- gate_weight: bfloat16 [128, 4096, 768], P(('ctx', 'dp')), may hold values from -0.09375 to 0.09375
- up_weight: bfloat16 [128, 4096, 768], P(('ctx', 'dp')), may hold values from -0.09375 to 0.09375
- down_weight: bfloat16 [128, 768, 4096], P(('ctx', 'dp')), may hold values from -0.15625 to 0.15625
Outputs:
- mixed: bfloat16 [1024, 4096], P(('ctx', 'dp'))
- gate_grads: float32 [1024, 8], P(('ctx', 'dp'))
- token_grads: bfloat16 [1024, 4096], P(('ctx', 'dp'))
Inputs may be any that keep to these rules, and one draw needn't show every extreme that they name: `expert_ids`: each row names 8 different experts. Among the rows of one device each expert is named by either no row or exactly 2 rows, and every expert is named by exactly 2 rows on some device.
All inputs are finite; a program needn't handle non-finite values.
Results may differ from a plain program's by a relative error of at most 0.0065.
Values may be sent and summed in bfloat16 or wider, within the bound.
A program may use at most 128 MiB of HBM per device.

v0:
```python
import functools

import jax
import jax.numpy as jnp
from jax import lax
from jax.experimental import pallas as pl
from jax.experimental.pallas import tpu as pltpu
from jax.sharding import PartitionSpec as P

MESH = pl.DeviceIdType.MESH
BF16 = jnp.bfloat16
F32 = jnp.float32
LANES = 128
RING = 4
EXPERTS = 64
SLOTS = 256
HIDDEN = 768
WIDTH = 4096

ORDERS = ((2, 1, 0), (0, 2, 1), (1, 0, 2))
STARTS = (0, 1408, 2816)
WIDTHS = (1408, 1408, 1280)
TOP = 768
LOWS = (640, 640, 512)
LOW = 640
CARRIED = TOP + LOW
PARTS = range(3)


def device_at(place, core):
    x, y, z = place
    return (x * 4 + (z % 2) * 2 + core, (z // 2) * 4 + y)


def expert_at(place, core):
    x, y, z = place
    return x * 16 + (z % 2) * 8 + core * 4 + (z // 2) * 2 + y // 2


def moved(place, axis, value):
    return tuple(value if i == axis else place[i] for i in range(3))


def iota(shape, axis):
    return lax.broadcasted_iota(jnp.int32, shape, axis)


def dot(a, b):
    return jnp.dot(a, b, preferred_element_type=F32)


def dot_nt(a, b):
    return lax.dot_general(a, b, (((1,), (1,)), ((), ())), preferred_element_type=F32)


def blocks(width, size):
    return [(i, min(size, width - i)) for i in range(0, width, size)]


def slot_coordinates(index, part):
    first, middle, last = ORDERS[part]
    coords = [None] * 3
    coords[last] = index // 64
    coords[middle] = (index // 8) % 4
    coords[first] = (index // 2) % 4
    return coords, (index // 32) % 2, index % 2


def index_in(part, coords, core, slot):
    first, middle, last = ORDERS[part]
    return coords[last] * 64 + core * 32 + coords[middle] * 8 + coords[first] * 2 + slot


def reorder(part, back):
    rows, cols = iota((SLOTS, SLOTS), 0), iota((SLOTS, SLOTS), 1)
    mine, other = (cols, rows) if back else (rows, cols)
    coords, core, slot = slot_coordinates(mine, part)
    return (index_in(0, coords, core, slot) == other).astype(F32).astype(BF16)


def kernel(
    tokens_hbm, cotangent_hbm, ids_hbm, gates_hbm, gate_hbm, up_hbm, down_hbm,
    mixed_ref, gate_grads_ref, token_grads_ref,
    tokens_ref, cotangent_ref, ids_ref, gates_ref, gate_w, up_w, down_w,
    token_rows, grad_rows, token_send, token_recv, grad_send, grad_recv,
    act, out_send, out_recv, in_send, in_recv,
    out_mid, out_mid_recv, in_mid, in_mid_recv, end_send, end_recv,
    input_sem, weight_sem,
    s1_send, s1_recv, s2_send, s2_recv, t3_send, t3_recv, c3_send, c3_recv,
    m3_send, m3_recv, g3_send, g3_recv, m2_send, m2_recv, g2_send, g2_recv, e1_send, e1_recv,
):
    ctx, dp = lax.axis_index("ctx"), lax.axis_index("dp")
    place = (ctx // 4, dp % 4, (dp // 4) * 2 + (ctx // 2) % 2)
    core = ctx % 2
    expert = expert_at(place, core)

    barrier = pltpu.get_barrier_semaphore()
    peers = [(place, 1 - core)]
    for axis in range(3):
        for offset in range(1, RING):
            there = moved(place, axis, (place[axis] + offset) % RING)
            peers += [(there, core), (there, 1 - core)]
    for there, its_core in peers:
        pl.semaphore_signal(
            barrier, inc=1, device_id=device_at(there, its_core), device_id_type=MESH
        )

    inputs = [
        pltpu.make_async_copy(src, dst, input_sem.at[i])
        for i, (src, dst) in enumerate(
            (
                (ids_hbm, ids_ref),
                (gates_hbm, gates_ref),
                (tokens_hbm, tokens_ref),
                (cotangent_hbm, cotangent_ref),
            )
        )
    ]
    for load in inputs:
        load.start()
    loads = [
        pltpu.make_async_copy(src.at[0], dst, weight_sem.at[i])
        for i, (src, dst) in enumerate(((gate_hbm, gate_w), (up_hbm, up_w), (down_hbm, down_w)))
    ]

    inputs[0].wait()
    inputs[1].wait()
    lane = iota((8, LANES), 1)
    named = jnp.zeros((8, LANES), F32)
    gate = jnp.zeros((8, LANES), F32)
    for k in range(8):
        hit = ids_ref[:, k : k + 1] == lane % EXPERTS
        named = jnp.where(hit, 1.0, named)
        gate = jnp.where(hit, gates_ref[:, k : k + 1], gate)
    row = iota((8, LANES), 0)
    before = jnp.zeros((8, LANES), F32)
    for i in range(7):
        before = before + jnp.where(row > i, named[i : i + 1, :], 0.0)
    slots = jnp.where(before == (lane // EXPERTS).astype(F32), named, 0.0)
    gate_high = gate.astype(BF16).astype(F32)
    gate_tile = jnp.where(lane < EXPERTS, gate_high, gate - gate_high)

    def stacked(ref, p, tiles):
        cut = STARTS[p] + TOP
        top = ref[:, STARTS[p] : cut].astype(F32)
        low = ref[:, cut : cut + LOWS[p]].astype(F32)
        return jnp.concatenate((top, jnp.concatenate((low, *tiles), axis=1)), axis=0).astype(BF16)

    inputs[2].wait()
    for p in PARTS:
        first, middle, last = ORDERS[p]
        tiles = (gate_tile, slots) if p == 2 else (slots,)
        token_rows[p, place[middle], place[first]] = stacked(tokens_ref, p, tiles)
    inputs[3].wait()
    for p in PARTS:
        first, middle, last = ORDERS[p]
        blank = jnp.zeros((8, TOP - LOWS[p]), F32)
        grad_rows[p, place[middle], place[first]] = stacked(cotangent_ref, p, (blank,))

    pl.semaphore_wait(barrier, len(peers))

    def taken(ref, sem):
        pltpu.make_async_copy(ref, ref, sem).wait()

    def ring(axis, source, target, send_sem, recv_sem):
        for offset in range(1, RING):
            there = moved(place, axis, (place[axis] + offset) % RING)
            pltpu.make_async_remote_copy(
                src_ref=source(there[axis]),
                dst_ref=target(offset),
                send_sem=send_sem,
                recv_sem=recv_sem,
                device_id=device_at(there, core),
                device_id_type=MESH,
            ).start()

    def exchange(axis, source, target, send_sem, recv_sem):
        mine = target.at[2 * place[axis] + core]
        for offset in (2, 1, 3, 0):
            there = moved(place, axis, (place[axis] + offset) % RING)
            for flip in range(2):
                its_core = core if flip == 0 else 1 - core
                block = source.at[2 * there[axis] + its_core]
                if offset == 0 and flip == 0:
                    pltpu.make_async_copy(block, mine, recv_sem).start()
                    continue
                pltpu.make_async_remote_copy(
                    src_ref=block,
                    dst_ref=mine,
                    send_sem=send_sem,
                    recv_sem=recv_sem,
                    device_id=device_at(there, its_core),
                    device_id_type=MESH,
                ).start()

    kinds = (token_rows, grad_rows)
    for kind, rows in enumerate(kinds):
        for p in PARTS:
            first, middle, last = ORDERS[p]
            home = rows.at[p, place[middle], place[first]]
            ring(
                first, lambda there: home, lambda offset: home,
                s1_send.at[kind], s1_recv.at[kind, p],
            )
    for load in loads:
        load.start()
    for kind, rows in enumerate(kinds):
        for p in PARTS:
            first, middle, last = ORDERS[p]
            home = rows.at[p, place[middle]]
            taken(rows.at[p, 0, pl.ds(0, 3)], s1_recv.at[kind, p])
            ring(
                middle, lambda there: home, lambda offset: home,
                s2_send.at[kind], s2_recv.at[kind, p],
            )

    r0, r1 = iota((SLOTS, SLOTS), 0), iota((SLOTS, SLOTS), 1)
    same = (r0 // 2) % 16 == r1 // 16
    half_masks = [same & ((r1 // 8) % 2 == h) for h in range(2)]
    u0, u1 = iota((SLOTS // 2, SLOTS), 0), iota((SLOTS // 2, SLOTS), 1)
    same_back = u0 // 8 == (u1 // 2) % 16
    lane = iota((SLOTS, LANES), 1)
    to_home, picks = [], []

    def pick_rows(p, h, rows, out, base, width):
        for start, size in blocks(width, 256):
            part = rows[p, :, :, :, start : start + size].reshape(SLOTS, size)
            out[:, :, base + start : base + start + size] = (
                dot(picks[p][h], part).astype(BF16).reshape(8, 32, size)
            )

    for p in PARTS:
        first, middle, last = ORDERS[p]
        taken(token_rows.at[p, pl.ds(0, 3)], s2_recv.at[0, p])
        index = iota((SLOTS, LANES), 0)
        wanted = expert_at(moved(place, last, index // 64), (index // 32) % 2)
        pick = (lane == (index % 2) * EXPERTS + wanted).astype(F32).astype(BF16)
        tile = token_rows[p, :, :, :, LOW:TOP].reshape(SLOTS, LANES)
        tile = tile.astype(F32).reshape(16, 2, 8, LANES)[:, 1]
        twice = jnp.concatenate((tile, tile), axis=1).reshape(SLOTS, LANES).astype(BF16)
        chosen = dot_nt(pick, twice)
        picks.append([jnp.where(mask, chosen, 0.0).astype(BF16) for mask in half_masks])
        home = dot_nt(tile.reshape(SLOTS // 2, LANES).astype(BF16), pick)
        to_home.append(jnp.where(same_back, home, 0.0).astype(BF16))
        pick_rows(p, 0, token_rows, token_send[0].at[p], 0, TOP)
        exchange(
            last, token_send[0].at[p], token_recv[0].at[p], t3_send.at[0], t3_recv.at[0, p]
        )
    for p in PARTS:
        pick_rows(p, 1, token_rows, token_send[1].at[p], 0, LOW)
        exchange(
            ORDERS[p][2], token_send[1].at[p], token_recv[1].at[p],
            t3_send.at[1], t3_recv.at[1, p],
        )
    for p in PARTS:
        taken(grad_rows.at[p, pl.ds(0, 3)], s2_recv.at[1, p])
        pick_rows(p, 0, grad_rows, grad_send.at[p], 0, TOP)
        pick_rows(p, 1, grad_rows, grad_send.at[p], TOP, LOW)
        exchange(
            ORDERS[p][2], grad_send.at[p], grad_recv.at[p], c3_send.at[0], c3_recv.at[p]
        )

    def in_order(p, rows):
        return rows if p == 0 else dot(reorder(p, True), rows).astype(BF16)

    gate_slot = None
    loads[0].wait()
    loads[1].wait()
    for h in range(2):
        for p in PARTS:
            taken(token_recv[h].at[p], t3_recv.at[h, p])
            rows = in_order(p, token_recv[h][p].reshape(SLOTS, (TOP, LOW)[h]))
            size = (TOP, LOWS[p])[h]
            if h == 1 and p == 2:
                tile = rows[:, size:].astype(F32)
                gate_slot = jnp.sum(
                    jnp.where(lane % EXPERTS == expert, tile, 0.0), axis=1, keepdims=True
                )
                rows = rows[:, :size]
            begin = STARTS[p] + h * TOP
            for i, weight in enumerate((gate_w, up_w)):
                for start, width in blocks(HIDDEN, 256):
                    value = dot(rows, weight[begin : begin + size, start : start + width])
                    if h == 0 and p == 0:
                        act[i, :, start : start + width] = value
                    else:
                        act[i, :, start : start + width] += value
    gate_act, second = act[0], act[1]
    squash = jax.nn.sigmoid(gate_act)
    hidden = gate_act * squash * second
    hidden_gated = (gate_slot * hidden).astype(BF16)
    act[2] = hidden
    loads[2].wait()

    def sent_order(p, value):
        return value if p == 0 else dot(reorder(p, False), value).astype(BF16)

    for p in PARTS:
        rows = sent_order(p, hidden_gated)
        for start, size in blocks(WIDTHS[p], 256):
            at = STARTS[p] + start
            out_send[p, :, :, start : start + size] = (
                dot(rows, down_w[:, at : at + size]).astype(BF16).reshape(8, 32, size)
            )
        if p == 2:
            out_send[p, :, :, WIDTHS[p] :] = jnp.zeros((8, 32, LANES), BF16)
        exchange(ORDERS[p][2], out_send.at[p], out_recv.at[p], m3_send.at[0], m3_recv.at[p])

    for p in PARTS:
        taken(grad_recv.at[p], c3_recv.at[p])
        rows = in_order(p, grad_recv[p, :, :, : WIDTHS[p]].reshape(SLOTS, WIDTHS[p]))
        feats = slice(STARTS[p], STARTS[p] + WIDTHS[p])
        for start, size in blocks(HIDDEN, 256):
            value = dot_nt(rows, down_w[start : start + size, feats])
            if p == 0:
                act[3, :, start : start + size] = value
            else:
                act[3, :, start : start + size] += value
    backward = act[3]
    gate_act, second = act[0], act[1]
    squash = jax.nn.sigmoid(gate_act)
    gate_grad = jnp.sum(backward * act[2], axis=1, keepdims=True)
    scaled = backward * gate_slot * squash
    grad_gate = (scaled * second * (1.0 + gate_act * (1.0 - squash))).astype(BF16)
    grad_second = (scaled * gate_act).astype(BF16)
    grad_high = gate_grad.astype(BF16).astype(F32)
    grad_tile = jnp.where(
        lane == expert, grad_high, jnp.where(lane == expert + EXPERTS, gate_grad - grad_high, 0.0)
    ).astype(BF16)
    sent_gate = [sent_order(p, grad_gate) for p in PARTS]
    sent_second = [sent_order(p, grad_second) for p in PARTS]

    def send_gradients(h):
        for p in PARTS:
            width = (TOP, LOWS[p])[h]
            for start, size in blocks(width, 256):
                at = STARTS[p] + h * TOP + start
                value = dot_nt(sent_gate[p], gate_w[at : at + size, :]) + dot_nt(
                    sent_second[p], up_w[at : at + size, :]
                )
                in_send[h][p, :, :, start : start + size] = value.astype(BF16).reshape(8, 32, size)
            if h == 1 and p == 2:
                in_send[h][p, :, :, width:] = sent_order(p, grad_tile).reshape(8, 32, LANES)
            exchange(
                ORDERS[p][2], in_send[h].at[p], in_recv[h].at[p],
                g3_send.at[h], g3_recv.at[h, p],
            )

    def to_middle(p, recv, mid, mid_recv, width, sem, send_sem, recv_sem):
        taken(recv, sem)
        for start, size in blocks(width, 256):
            rows = recv[:, :, start : start + size].reshape(SLOTS, size)
            mid[:, :, start : start + size] = (
                dot(to_home[p], rows).astype(BF16).reshape(RING, 32, size)
            )
        ring(
            ORDERS[p][1], lambda there: mid.at[there], lambda offset: mid_recv.at[offset - 1],
            send_sem, recv_sem,
        )

    def middle_sum(p, mid, mid_recv, sem):
        taken(mid_recv, sem)
        value = mid[place[ORDERS[p][1]]].astype(F32)
        for i in range(3):
            value = value + mid_recv[i].astype(F32)
        return value.reshape(RING, 8, value.shape[-1])

    def to_end(kind, p, top, low):
        send = end_send.at[kind, p]
        send[:, :, :LOW] = jnp.concatenate((top[:, :, :LOW], low), axis=1).astype(BF16)
        rest = top[:, :, LOW:]
        send[:, :, LOW:] = jnp.concatenate((rest, jnp.zeros_like(rest)), axis=1).astype(BF16)
        ring(
            ORDERS[p][0], lambda there: send.at[there],
            lambda offset: end_recv.at[kind, p, offset - 1],
            e1_send.at[kind], e1_recv.at[kind, p],
        )

    send_gradients(0)
    for p in PARTS:
        to_middle(
            p, out_recv.at[p], out_mid.at[p], out_mid_recv.at[p], CARRIED,
            m3_recv.at[p], m2_send.at[0], m2_recv.at[p],
        )
    send_gradients(1)
    for h in range(2):
        for p in PARTS:
            to_middle(
                p, in_recv[h].at[p], in_mid[h].at[p], in_mid_recv[h].at[p], (TOP, LOW)[h],
                g3_recv.at[h, p], g2_send.at[h], g2_recv.at[h, p],
            )
        if h == 0:
            for p in PARTS:
                value = middle_sum(p, out_mid.at[p], out_mid_recv.at[p], m2_recv.at[p])
                to_end(0, p, value[:, :, :TOP], value[:, :, TOP:])
    tops = [
        middle_sum(p, in_mid[0].at[p], in_mid_recv[0].at[p], g2_recv.at[0, p]) for p in PARTS
    ]
    for p in PARTS:
        low = middle_sum(p, in_mid[1].at[p], in_mid_recv[1].at[p], g2_recv.at[1, p])
        to_end(1, p, tops[p], low)

    for kind, out_ref in enumerate((mixed_ref, token_grads_ref)):
        for p in PARTS:
            taken(end_recv.at[kind, p], e1_recv.at[kind, p])
            value = end_send[kind, p, place[ORDERS[p][0]]].astype(F32)
            for i in range(3):
                value = value + end_recv[kind, p, i].astype(F32)
            cut = STARTS[p] + TOP
            out_ref[:, STARTS[p] : cut] = value[:8].astype(BF16)
            out_ref[:, cut : cut + LOWS[p]] = value[8:, : LOWS[p]].astype(BF16)
            if kind == 1 and p == 2:
                tile = value[8:, LOWS[p] : LOW]
                lane8 = iota((8, LANES), 1)
                column = iota((8, 8), 1)
                grads = jnp.zeros((8, 8), F32)
                for k in range(8):
                    hit = ids_ref[:, k : k + 1] == lane8 % EXPERTS
                    picked = jnp.sum(jnp.where(hit, tile, 0.0), axis=1, keepdims=True)
                    grads = jnp.where(column == k, picked, grads)
                gate_grads_ref[...] = grads

    for kind, rows in enumerate(kinds):
        taken(rows.at[:, 0, pl.ds(0, 3)], s1_send.at[kind])
        taken(rows.at[:, pl.ds(0, 3)], s2_send.at[kind])
        taken(end_send.at[kind, :, pl.ds(0, 3)], e1_send.at[kind])
    for h in range(2):
        taken(token_send[h].at[:, pl.ds(0, 7)], t3_send.at[h])
        taken(in_send[h].at[:, pl.ds(0, 7)], g3_send.at[h])
        taken(in_mid[h].at[:, pl.ds(0, 3)], g2_send.at[h])
    taken(grad_send.at[:, pl.ds(0, 7)], c3_send.at[0])
    taken(out_send.at[:, pl.ds(0, 7)], m3_send.at[0])
    taken(out_mid.at[:, pl.ds(0, 3)], m2_send.at[0])


def hand_over(*refs):
    for source, target in zip(refs[:3], refs[3:]):
        target[...] = source[...]


def shards(tokens, cotangent, expert_ids, gates, gate_weight, up_weight, down_weight):
    def vmem(shape, dtype=BF16):
        return pltpu.VMEM(shape, dtype)

    def parts(shape, widths, dtype=BF16):
        return [vmem((*shape, width), dtype) for width in widths]

    dma = pltpu.SemaphoreType.DMA
    block = (3, 8, 32)
    halves = (TOP, LOW)
    whole = pl.BlockSpec(memory_space=pltpu.VMEM)
    hbm = pl.BlockSpec(memory_space=pl.ANY)
    out_shape = (
        jax.ShapeDtypeStruct((8, WIDTH), BF16),
        jax.ShapeDtypeStruct((8, 8), F32),
        jax.ShapeDtypeStruct((8, WIDTH), BF16),
    )
    results = pl.pallas_call(
        kernel,
        out_shape=out_shape,
        in_specs=[hbm] * 7,
        out_specs=[whole] * 3,
        scratch_shapes=[
            vmem((8, WIDTH)),
            vmem((8, WIDTH)),
            vmem((8, 8), jnp.int32),
            vmem((8, 8), F32),
            vmem((WIDTH, HIDDEN)),
            vmem((WIDTH, HIDDEN)),
            vmem((HIDDEN, WIDTH)),
            vmem((3, RING, RING, 16, TOP)),
            vmem((3, RING, RING, 16, TOP)),
            parts(block, halves),
            parts(block, halves),
            vmem((*block, CARRIED)),
            vmem((*block, CARRIED)),
            vmem((4, SLOTS, HIDDEN), F32),
            vmem((*block, CARRIED)),
            vmem((*block, CARRIED)),
            parts(block, halves),
            parts(block, halves),
            vmem((3, RING, 32, CARRIED)),
            vmem((3, RING - 1, 32, CARRIED)),
            parts((3, RING, 32), halves),
            parts((3, RING - 1, 32), halves),
            vmem((2, 3, RING, 16, TOP)),
            vmem((2, 3, RING - 1, 16, TOP)),
            dma((4,)),
            dma((3,)),
            dma((2,)), dma((2, 3)), dma((2,)), dma((2, 3)),
            dma((2,)), dma((2, 3)), dma((1,)), dma((3,)),
            dma((1,)), dma((3,)), dma((2,)), dma((2, 3)),
            dma((1,)), dma((3,)), dma((2,)), dma((2, 3)),
            dma((2,)), dma((2, 3)),
        ],
        compiler_params=pltpu.CompilerParams(
            collective_id=0, has_side_effects=True, vmem_limit_bytes=60 * 2**20
        ),
    )(tokens, cotangent, expert_ids, gates, gate_weight, up_weight, down_weight)
    return pl.pallas_call(
        hand_over,
        out_shape=out_shape,
        in_specs=[whole] * 3,
        out_specs=[whole] * 3,
    )(*results)


def solution(mesh):
    rows = P(("ctx", "dp"), None)
    weights = P(("ctx", "dp"), None, None)
    return jax.shard_map(
        shards,
        mesh=mesh,
        in_specs=(rows, rows, rows, rows, weights, weights, weights),
        out_specs=(rows, rows, rows),
        check_vma=False,
    )
```

profile of v0, /device:TPU:1, one launch (start us, length us, event | category | flops | bytes accessed | tf_op | source)
XLA Modules:
  0.0 71.2 jit_solution(14799331200060144912)
XLA Ops:
  0.6 69.0 %shard_map.94 = (bf16[8,4096]{1,0:T(8,128)(2,1)}, f32[8,8]{1,0:T(8,128)}, bf16[8,4096]{1,0:T(8,128)(2,1)}) custom-call(bf16[8,4096]{1,0:T(8,128)(2,1)} %tokens_hbm.1, bf16[8,4096]{1,0:T(8,128)(2,1)} %cotangent_hbm.1, s32[8,8]{1,0:T(8,128)} %ids_hbm.1, f32[8,8]{1,0:T(8,128)} %gates_hbm.1, bf16[1,4096,768]{2,1,0:T(8,128)(2,1)} %gate_hbm.1, ...), custom_call_target="tpu_custom_call" | custom-call | tf_op jit(solution)/shard_map/pallas_call | solution.py:458
  69.7 1.5 %shard_map.95 = (bf16[8,4096]{1,0:T(8,128)(2,1)}, f32[8,8]{1,0:T(8,128)}, bf16[8,4096]{1,0:T(8,128)(2,1)}) custom-call(bf16[8,4096]{1,0:T(8,128)(2,1)} %get-tuple-element.6.refs_0_, f32[8,8]{1,0:T(8,128)} %get-tuple-element.7.refs_1_, bf16[8,4096]{1,0:T(8,128)(2,1)} %get-tuple-element.8.refs_2_), custom_call_target="tpu_custom_call" | custom-call | tf_op jit(solution)/shard_map/pallas_call | solution.py:500
where the time goes:
time: 71.4 us; the launch traced here: 71.2 us
  Pallas kernels  70.5 us (99%)
    pallas_call x1, Pallas kernels, shards(): pl.pallas_call(kernel, out_shape=out_shape, in_specs=[hbm] * 7, out_specs...  69 us
    pallas_call x1, Pallas kernels, shards(): pl.pallas_call(hand_over, out_shape=out_shape, in_specs=[whole] * 3, out_...  1.53 us

commit v1 on v0

--- a/solution.py
+++ b/solution.py
@@ -24,6 +24,7 @@
 LOWS = (640, 640, 512)
 LOW = 640
 CARRIED = TOP + LOW
+END = TOP // 2
 PARTS = range(3)
 
 
@@ -295,16 +296,23 @@
     def sent_order(p, value):
         return value if p == 0 else dot(reorder(p, False), value).astype(BF16)
 
-    for p in PARTS:
-        rows = sent_order(p, hidden_gated)
-        for start, size in blocks(WIDTHS[p], 256):
-            at = STARTS[p] + start
-            out_send[p, :, :, start : start + size] = (
-                dot(rows, down_w[:, at : at + size]).astype(BF16).reshape(8, 32, size)
-            )
-        if p == 2:
-            out_send[p, :, :, WIDTHS[p] :] = jnp.zeros((8, 32, LANES), BF16)
-        exchange(ORDERS[p][2], out_send.at[p], out_recv.at[p], m3_send.at[0], m3_recv.at[p])
+    hidden_sent = [sent_order(p, hidden_gated) for p in PARTS]
+    for h in range(2):
+        for p in PARTS:
+            width = (TOP, LOWS[p])[h]
+            for start, size in blocks(width, 256):
+                at = STARTS[p] + h * TOP + start
+                out_send[h][p, :, :, start : start + size] = (
+                    dot(hidden_sent[p], down_w[:, at : at + size])
+                    .astype(BF16)
+                    .reshape(8, 32, size)
+                )
+            if h == 1 and p == 2:
+                out_send[h][p, :, :, width:] = jnp.zeros((8, 32, LANES), BF16)
+            exchange(
+                ORDERS[p][2], out_send[h].at[p], out_recv[h].at[p],
+                m3_send.at[h], m3_recv.at[h, p],
+            )
 
     for p in PARTS:
         taken(grad_recv.at[p], c3_recv.at[p])
@@ -346,13 +354,15 @@
                 g3_send.at[h], g3_recv.at[h, p],
             )
 
-    def to_middle(p, recv, mid, mid_recv, width, sem, send_sem, recv_sem):
+    def slot_sum(p, recv, mid, width, sem):
         taken(recv, sem)
         for start, size in blocks(width, 256):
             rows = recv[:, :, start : start + size].reshape(SLOTS, size)
             mid[:, :, start : start + size] = (
                 dot(to_home[p], rows).astype(BF16).reshape(RING, 32, size)
             )
+
+    def to_middle(p, mid, mid_recv, send_sem, recv_sem):
         ring(
             ORDERS[p][1], lambda there: mid.at[there], lambda offset: mid_recv.at[offset - 1],
             send_sem, recv_sem,
@@ -365,71 +375,90 @@
             value = value + mid_recv[i].astype(F32)
         return value.reshape(RING, 8, value.shape[-1])
 
-    def to_end(kind, p, top, low):
+    def end_pack(kind, p, h, value):
+        rest = value[:, :, END:]
+        if h == 1:
+            rest = jnp.concatenate((rest, jnp.zeros((RING, 8, TOP - LOW), F32)), axis=2)
+        end_send[kind, p, :, :, h * END : (h + 1) * END] = jnp.concatenate(
+            (value[:, :, :END], rest), axis=1
+        ).astype(BF16)
+
+    def to_end(kind, p, cols, send_sem, recv_sem):
         send = end_send.at[kind, p]
-        send[:, :, :LOW] = jnp.concatenate((top[:, :, :LOW], low), axis=1).astype(BF16)
-        rest = top[:, :, LOW:]
-        send[:, :, LOW:] = jnp.concatenate((rest, jnp.zeros_like(rest)), axis=1).astype(BF16)
         ring(
-            ORDERS[p][0], lambda there: send.at[there],
-            lambda offset: end_recv.at[kind, p, offset - 1],
-            e1_send.at[kind], e1_recv.at[kind, p],
-        )
-
+            ORDERS[p][0], lambda there: send.at[there, :, cols],
+            lambda offset: end_recv.at[kind, p, offset - 1, :, cols], send_sem, recv_sem,
+        )
+
+    end_cols = (pl.ds(0, END), pl.ds(END, END))
     send_gradients(0)
-    for p in PARTS:
-        to_middle(
-            p, out_recv.at[p], out_mid.at[p], out_mid_recv.at[p], CARRIED,
-            m3_recv.at[p], m2_send.at[0], m2_recv.at[p],
-        )
     send_gradients(1)
     for h in range(2):
         for p in PARTS:
-            to_middle(
-                p, in_recv[h].at[p], in_mid[h].at[p], in_mid_recv[h].at[p], (TOP, LOW)[h],
-                g3_recv.at[h, p], g2_send.at[h], g2_recv.at[h, p],
-            )
+            mid = in_mid[h].at[p]
+            slot_sum(p, in_recv[h].at[p], mid, (TOP, LOW)[h], g3_recv.at[h, p])
+            to_middle(p, mid, in_mid_recv[h].at[p], g2_send.at[h], g2_recv.at[h, p])
         if h == 0:
             for p in PARTS:
-                value = middle_sum(p, out_mid.at[p], out_mid_recv.at[p], m2_recv.at[p])
-                to_end(0, p, value[:, :, :TOP], value[:, :, TOP:])
-    tops = [
-        middle_sum(p, in_mid[0].at[p], in_mid_recv[0].at[p], g2_recv.at[0, p]) for p in PARTS
-    ]
-    for p in PARTS:
-        low = middle_sum(p, in_mid[1].at[p], in_mid_recv[1].at[p], g2_recv.at[1, p])
-        to_end(1, p, tops[p], low)
-
-    for kind, out_ref in enumerate((mixed_ref, token_grads_ref)):
-        for p in PARTS:
-            taken(end_recv.at[kind, p], e1_recv.at[kind, p])
-            value = end_send[kind, p, place[ORDERS[p][0]]].astype(F32)
-            for i in range(3):
-                value = value + end_recv[kind, p, i].astype(F32)
-            cut = STARTS[p] + TOP
-            out_ref[:, STARTS[p] : cut] = value[:8].astype(BF16)
-            out_ref[:, cut : cut + LOWS[p]] = value[8:, : LOWS[p]].astype(BF16)
-            if kind == 1 and p == 2:
-                tile = value[8:, LOWS[p] : LOW]
-                lane8 = iota((8, LANES), 1)
-                column = iota((8, 8), 1)
-                grads = jnp.zeros((8, 8), F32)
-                for k in range(8):
-                    hit = ids_ref[:, k : k + 1] == lane8 % EXPERTS
-                    picked = jnp.sum(jnp.where(hit, tile, 0.0), axis=1, keepdims=True)
-                    grads = jnp.where(column == k, picked, grads)
-                gate_grads_ref[...] = grads
+                for i in range(2):
+                    width = (TOP, LOW)[i]
+                    mid = out_mid.at[p, :, :, pl.ds(i * TOP, width)]
+                    slot_sum(p, out_recv[i].at[p], mid, width, m3_recv.at[i, p])
+                to_middle(p, out_mid.at[p], out_mid_recv.at[p], m2_send.at[0], m2_recv.at[p])
+
+    def end_gradients(h):
+        for p in PARTS:
+            value = middle_sum(p, in_mid[h].at[p], in_mid_recv[h].at[p], g2_recv.at[h, p])
+            end_pack(1, p, h, value)
+            to_end(1, p, end_cols[h], e1_send.at[h], e1_recv.at[h, p])
+
+    end_gradients(0)
+    for p in PARTS:
+        value = middle_sum(p, out_mid.at[p], out_mid_recv.at[p], m2_recv.at[p])
+        end_pack(0, p, 0, value[:, :, :TOP])
+        end_pack(0, p, 1, value[:, :, TOP:])
+        to_end(0, p, pl.ds(0, TOP), e1_send.at[2], e1_recv.at[2, p])
+    end_gradients(1)
+
+    def finish(kind, out_ref, p, h):
+        cols = end_cols[h]
+        value = end_send[kind, p, place[ORDERS[p][0]], :, cols].astype(F32)
+        for i in range(3):
+            value = value + end_recv[kind, p, i, :, cols].astype(F32)
+        begin = STARTS[p] + h * TOP
+        rest = (TOP, LOWS[p])[h] - END
+        out_ref[:, begin : begin + END] = value[:8].astype(BF16)
+        out_ref[:, begin + END : begin + END + rest] = value[8:, :rest].astype(BF16)
+        return value[8:, rest : rest + LANES]
+
+    for p in PARTS:
+        taken(end_recv.at[0, p], e1_recv.at[2, p])
+        for h in range(2):
+            finish(0, mixed_ref, p, h)
+    for h in range(2):
+        for p in PARTS:
+            taken(end_recv.at[1, p, :, :, end_cols[h]], e1_recv.at[h, p])
+            tile = finish(1, token_grads_ref, p, h)
+    lane8 = iota((8, LANES), 1)
+    column = iota((8, 8), 1)
+    grads = jnp.zeros((8, 8), F32)
+    for k in range(8):
+        hit = ids_ref[:, k : k + 1] == lane8 % EXPERTS
+        picked = jnp.sum(jnp.where(hit, tile, 0.0), axis=1, keepdims=True)
+        grads = jnp.where(column == k, picked, grads)
+    gate_grads_ref[...] = grads
 
     for kind, rows in enumerate(kinds):
         taken(rows.at[:, 0, pl.ds(0, 3)], s1_send.at[kind])
         taken(rows.at[:, pl.ds(0, 3)], s2_send.at[kind])
-        taken(end_send.at[kind, :, pl.ds(0, 3)], e1_send.at[kind])
     for h in range(2):
         taken(token_send[h].at[:, pl.ds(0, 7)], t3_send.at[h])
         taken(in_send[h].at[:, pl.ds(0, 7)], g3_send.at[h])
         taken(in_mid[h].at[:, pl.ds(0, 3)], g2_send.at[h])
+        taken(out_send[h].at[:, pl.ds(0, 7)], m3_send.at[h])
+        taken(end_send.at[1, :, pl.ds(0, 3), :, end_cols[h]], e1_send.at[h])
     taken(grad_send.at[:, pl.ds(0, 7)], c3_send.at[0])
-    taken(out_send.at[:, pl.ds(0, 7)], m3_send.at[0])
+    taken(end_send.at[0, :, pl.ds(0, 3)], e1_send.at[2])
     taken(out_mid.at[:, pl.ds(0, 3)], m2_send.at[0])
 
 
@@ -475,8 +504,8 @@
             vmem((*block, CARRIED)),
             vmem((*block, CARRIED)),
             vmem((4, SLOTS, HIDDEN), F32),
-            vmem((*block, CARRIED)),
-            vmem((*block, CARRIED)),
+            parts(block, halves),
+            parts(block, halves),
             parts(block, halves),
             parts(block, halves),
             vmem((3, RING, 32, CARRIED)),
@@ -489,9 +518,9 @@
             dma((3,)),
             dma((2,)), dma((2, 3)), dma((2,)), dma((2, 3)),
             dma((2,)), dma((2, 3)), dma((1,)), dma((3,)),
+            dma((2,)), dma((2, 3)), dma((2,)), dma((2, 3)),
             dma((1,)), dma((3,)), dma((2,)), dma((2, 3)),
-            dma((1,)), dma((3,)), dma((2,)), dma((2, 3)),
-            dma((2,)), dma((2, 3)),
+            dma((3,)), dma((3, 3)),
         ],
         compiler_params=pltpu.CompilerParams(
             collective_id=0, has_side_effects=True, vmem_limit_bytes=60 * 2**20

time: 71.4 us -> 70 us (0.980)
  Pallas kernels: 70.5 us -> 69.2 us
    pallas_call x1, Pallas kernels: 69 us -> 67.6 us  [shards(): pl.pallas_call(kernel, out_shape=out_shape, in_specs=[hbm] * 7, out_specs...]
where the time goes in v1:
time: 70 us; the launch traced here: 69.8 us
  Pallas kernels  69.2 us (99%)
    pallas_call x1, Pallas kernels, shards(): pl.pallas_call(kernel, out_shape=out_shape, in_specs=[hbm] * 7, out_specs...  67.6 us
    pallas_call x1, Pallas kernels, shards(): pl.pallas_call(hand_over, out_shape=out_shape, in_specs=[whole] * 3, out_...  1.53 us

profile of v1, /device:TPU:1, one launch (start us, length us, event | category | flops | bytes accessed | tf_op | source)
XLA Modules:
  0.0 69.8 jit_solution(10929811304640840131)
XLA Ops:
  0.6 67.6 %shard_map.94 = (bf16[8,4096]{1,0:T(8,128)(2,1)}, f32[8,8]{1,0:T(8,128)}, bf16[8,4096]{1,0:T(8,128)(2,1)}) custom-call(bf16[8,4096]{1,0:T(8,128)(2,1)} %tokens_hbm.1, bf16[8,4096]{1,0:T(8,128)(2,1)} %cotangent_hbm.1, s32[8,8]{1,0:T(8,128)} %ids_hbm.1, f32[8,8]{1,0:T(8,128)} %gates_hbm.1, bf16[1,4096,768]{2,1,0:T(8,128)(2,1)} %gate_hbm.1, ...), custom_call_target="tpu_custom_call" | custom-call | tf_op jit(solution)/shard_map/pallas_call | solution.py:487
  68.3 1.5 %shard_map.95 = (bf16[8,4096]{1,0:T(8,128)(2,1)}, f32[8,8]{1,0:T(8,128)}, bf16[8,4096]{1,0:T(8,128)(2,1)}) custom-call(bf16[8,4096]{1,0:T(8,128)(2,1)} %get-tuple-element.6.refs_0_, f32[8,8]{1,0:T(8,128)} %get-tuple-element.7.refs_1_, bf16[8,4096]{1,0:T(8,128)(2,1)} %get-tuple-element.8.refs_2_), custom_call_target="tpu_custom_call" | custom-call | tf_op jit(solution)/shard_map/pallas_call | solution.py:529

commit v2 on v1

--- a/solution.py
+++ b/solution.py
@@ -24,7 +24,8 @@
 LOWS = (640, 640, 512)
 LOW = 640
 CARRIED = TOP + LOW
-END = TOP // 2
+CUTS = ((512, 896), (768, 640), (896, 512))
+ENDS = ((256, 512), (384, 384))
 PARTS = range(3)
 
 
@@ -40,6 +41,10 @@
 
 def moved(place, axis, value):
     return tuple(value if i == axis else place[i] for i in range(3))
+
+
+def piece_width(kind, part, piece):
+    return CUTS[kind][0] if piece == 0 else WIDTHS[part] - CUTS[kind][0]
 
 
 def iota(shape, axis):
@@ -223,12 +228,24 @@
     lane = iota((SLOTS, LANES), 1)
     to_home, picks = [], []
 
-    def pick_rows(p, h, rows, out, base, width):
+    def pick_rows(p, h, rows, out, base, width, skip=0):
         for start, size in blocks(width, 256):
-            part = rows[p, :, :, :, start : start + size].reshape(SLOTS, size)
+            cols = slice(skip + start, skip + start + size)
+            part = rows[p, :, :, :, cols].reshape(SLOTS, size)
             out[:, :, base + start : base + start + size] = (
                 dot(picks[p][h], part).astype(BF16).reshape(8, 32, size)
             )
+
+    def pick_piece(p, piece):
+        begin = piece * CUTS[2][0]
+        end = begin + CUTS[2][piece]
+        for half, (low, high) in enumerate(((0, TOP), (TOP, CARRIED))):
+            left, right = max(begin, low), min(end, high)
+            if left < right:
+                pick_rows(
+                    p, half, token_rows, token_send[piece].at[p], left - begin, right - left,
+                    left - low,
+                )
 
     for p in PARTS:
         first, middle, last = ORDERS[p]
@@ -243,12 +260,12 @@
         picks.append([jnp.where(mask, chosen, 0.0).astype(BF16) for mask in half_masks])
         home = dot_nt(tile.reshape(SLOTS // 2, LANES).astype(BF16), pick)
         to_home.append(jnp.where(same_back, home, 0.0).astype(BF16))
-        pick_rows(p, 0, token_rows, token_send[0].at[p], 0, TOP)
+        pick_piece(p, 0)
         exchange(
             last, token_send[0].at[p], token_recv[0].at[p], t3_send.at[0], t3_recv.at[0, p]
         )
     for p in PARTS:
-        pick_rows(p, 1, token_rows, token_send[1].at[p], 0, LOW)
+        pick_piece(p, 1)
         exchange(
             ORDERS[p][2], token_send[1].at[p], token_recv[1].at[p],
             t3_send.at[1], t3_recv.at[1, p],
@@ -270,15 +287,15 @@
     for h in range(2):
         for p in PARTS:
             taken(token_recv[h].at[p], t3_recv.at[h, p])
-            rows = in_order(p, token_recv[h][p].reshape(SLOTS, (TOP, LOW)[h]))
-            size = (TOP, LOWS[p])[h]
+            rows = in_order(p, token_recv[h][p].reshape(SLOTS, CUTS[2][h]))
+            size = piece_width(2, p, h)
             if h == 1 and p == 2:
                 tile = rows[:, size:].astype(F32)
                 gate_slot = jnp.sum(
                     jnp.where(lane % EXPERTS == expert, tile, 0.0), axis=1, keepdims=True
                 )
                 rows = rows[:, :size]
-            begin = STARTS[p] + h * TOP
+            begin = STARTS[p] + h * CUTS[2][0]
             for i, weight in enumerate((gate_w, up_w)):
                 for start, width in blocks(HIDDEN, 256):
                     value = dot(rows, weight[begin : begin + size, start : start + width])
@@ -299,9 +316,9 @@
     hidden_sent = [sent_order(p, hidden_gated) for p in PARTS]
     for h in range(2):
         for p in PARTS:
-            width = (TOP, LOWS[p])[h]
+            width = piece_width(0, p, h)
             for start, size in blocks(width, 256):
-                at = STARTS[p] + h * TOP + start
+                at = STARTS[p] + h * CUTS[0][0] + start
                 out_send[h][p, :, :, start : start + size] = (
                     dot(hidden_sent[p], down_w[:, at : at + size])
                     .astype(BF16)
@@ -340,9 +357,9 @@
 
     def send_gradients(h):
         for p in PARTS:
-            width = (TOP, LOWS[p])[h]
+            width = piece_width(1, p, h)
             for start, size in blocks(width, 256):
-                at = STARTS[p] + h * TOP + start
+                at = STARTS[p] + h * CUTS[1][0] + start
                 value = dot_nt(sent_gate[p], gate_w[at : at + size, :]) + dot_nt(
                     sent_second[p], up_w[at : at + size, :]
                 )
@@ -375,12 +392,17 @@
             value = value + mid_recv[i].astype(F32)
         return value.reshape(RING, 8, value.shape[-1])
 
+    def end_cols(kind, h):
+        return slice(h * ENDS[kind][0], h * ENDS[kind][0] + ENDS[kind][h])
+
     def end_pack(kind, p, h, value):
-        rest = value[:, :, END:]
-        if h == 1:
-            rest = jnp.concatenate((rest, jnp.zeros((RING, 8, TOP - LOW), F32)), axis=2)
-        end_send[kind, p, :, :, h * END : (h + 1) * END] = jnp.concatenate(
-            (value[:, :, :END], rest), axis=1
+        size = ENDS[kind][h]
+        rest = value[:, :, size:]
+        if rest.shape[2] < size:
+            blank = jnp.zeros((RING, 8, size - rest.shape[2]), F32)
+            rest = jnp.concatenate((rest, blank), axis=2)
+        end_send[kind, p, :, :, end_cols(kind, h)] = jnp.concatenate(
+            (value[:, :, :size], rest), axis=1
         ).astype(BF16)
 
     def to_end(kind, p, cols, send_sem, recv_sem):
@@ -390,19 +412,18 @@
             lambda offset: end_recv.at[kind, p, offset - 1, :, cols], send_sem, recv_sem,
         )
 
-    end_cols = (pl.ds(0, END), pl.ds(END, END))
     send_gradients(0)
     send_gradients(1)
     for h in range(2):
         for p in PARTS:
             mid = in_mid[h].at[p]
-            slot_sum(p, in_recv[h].at[p], mid, (TOP, LOW)[h], g3_recv.at[h, p])
+            slot_sum(p, in_recv[h].at[p], mid, CUTS[1][h], g3_recv.at[h, p])
             to_middle(p, mid, in_mid_recv[h].at[p], g2_send.at[h], g2_recv.at[h, p])
         if h == 0:
             for p in PARTS:
                 for i in range(2):
-                    width = (TOP, LOW)[i]
-                    mid = out_mid.at[p, :, :, pl.ds(i * TOP, width)]
+                    width = CUTS[0][i]
+                    mid = out_mid.at[p, :, :, pl.ds(i * CUTS[0][0], width)]
                     slot_sum(p, out_recv[i].at[p], mid, width, m3_recv.at[i, p])
                 to_middle(p, out_mid.at[p], out_mid_recv.at[p], m2_send.at[0], m2_recv.at[p])
 
@@ -410,25 +431,27 @@
         for p in PARTS:
             value = middle_sum(p, in_mid[h].at[p], in_mid_recv[h].at[p], g2_recv.at[h, p])
             end_pack(1, p, h, value)
-            to_end(1, p, end_cols[h], e1_send.at[h], e1_recv.at[h, p])
+            to_end(1, p, end_cols(1, h), e1_send.at[h], e1_recv.at[h, p])
 
     end_gradients(0)
     for p in PARTS:
         value = middle_sum(p, out_mid.at[p], out_mid_recv.at[p], m2_recv.at[p])
-        end_pack(0, p, 0, value[:, :, :TOP])
-        end_pack(0, p, 1, value[:, :, TOP:])
-        to_end(0, p, pl.ds(0, TOP), e1_send.at[2], e1_recv.at[2, p])
+        end_pack(0, p, 0, value[:, :, : CUTS[0][0]])
+        end_pack(0, p, 1, value[:, :, CUTS[0][0] :])
+        to_end(0, p, slice(0, TOP), e1_send.at[2], e1_recv.at[2, p])
     end_gradients(1)
 
     def finish(kind, out_ref, p, h):
-        cols = end_cols[h]
+        cols = end_cols(kind, h)
         value = end_send[kind, p, place[ORDERS[p][0]], :, cols].astype(F32)
         for i in range(3):
             value = value + end_recv[kind, p, i, :, cols].astype(F32)
-        begin = STARTS[p] + h * TOP
-        rest = (TOP, LOWS[p])[h] - END
-        out_ref[:, begin : begin + END] = value[:8].astype(BF16)
-        out_ref[:, begin + END : begin + END + rest] = value[8:, :rest].astype(BF16)
+        begin = STARTS[p] + h * CUTS[kind][0]
+        size = ENDS[kind][h]
+        rest = piece_width(kind, p, h) - size
+        out_ref[:, begin : begin + size] = value[:8].astype(BF16)
+        if rest > 0:
+            out_ref[:, begin + size : begin + size + rest] = value[8:, :rest].astype(BF16)
         return value[8:, rest : rest + LANES]
 
     for p in PARTS:
@@ -437,7 +460,7 @@
             finish(0, mixed_ref, p, h)
     for h in range(2):
         for p in PARTS:
-            taken(end_recv.at[1, p, :, :, end_cols[h]], e1_recv.at[h, p])
+            taken(end_recv.at[1, p, :, :, end_cols(1, h)], e1_recv.at[h, p])
             tile = finish(1, token_grads_ref, p, h)
     lane8 = iota((8, LANES), 1)
     column = iota((8, 8), 1)
@@ -456,7 +479,7 @@
         taken(in_send[h].at[:, pl.ds(0, 7)], g3_send.at[h])
         taken(in_mid[h].at[:, pl.ds(0, 3)], g2_send.at[h])
         taken(out_send[h].at[:, pl.ds(0, 7)], m3_send.at[h])
-        taken(end_send.at[1, :, pl.ds(0, 3), :, end_cols[h]], e1_send.at[h])
+        taken(end_send.at[1, :, pl.ds(0, 3), :, end_cols(1, h)], e1_send.at[h])
     taken(grad_send.at[:, pl.ds(0, 7)], c3_send.at[0])
     taken(end_send.at[0, :, pl.ds(0, 3)], e1_send.at[2])
     taken(out_mid.at[:, pl.ds(0, 3)], m2_send.at[0])
@@ -476,7 +499,6 @@
 
     dma = pltpu.SemaphoreType.DMA
     block = (3, 8, 32)
-    halves = (TOP, LOW)
     whole = pl.BlockSpec(memory_space=pltpu.VMEM)
     hbm = pl.BlockSpec(memory_space=pl.ANY)
     out_shape = (
@@ -499,19 +521,19 @@
             vmem((HIDDEN, WIDTH)),
             vmem((3, RING, RING, 16, TOP)),
             vmem((3, RING, RING, 16, TOP)),
-            parts(block, halves),
-            parts(block, halves),
+            parts(block, CUTS[2]),
+            parts(block, CUTS[2]),
             vmem((*block, CARRIED)),
             vmem((*block, CARRIED)),
             vmem((4, SLOTS, HIDDEN), F32),
-            parts(block, halves),
-            parts(block, halves),
-            parts(block, halves),
-            parts(block, halves),
+            parts(block, CUTS[0]),
+            parts(block, CUTS[0]),
+            parts(block, CUTS[1]),
+            parts(block, CUTS[1]),
             vmem((3, RING, 32, CARRIED)),
             vmem((3, RING - 1, 32, CARRIED)),
-            parts((3, RING, 32), halves),
-            parts((3, RING - 1, 32), halves),
+            parts((3, RING, 32), CUTS[1]),
+            parts((3, RING - 1, 32), CUTS[1]),
             vmem((2, 3, RING, 16, TOP)),
             vmem((2, 3, RING - 1, 16, TOP)),
             dma((4,)),

time: 70 us -> 69.6 us (level)
  no operation moved by 1% of the time
where the time goes in v2:
time: 69.6 us; the launch traced here: 69.4 us
  Pallas kernels  68.7 us (99%)
    pallas_call x1, Pallas kernels, shards(): pl.pallas_call(kernel, out_shape=out_shape, in_specs=[hbm] * 7, out_specs...  67.2 us
    pallas_call x1, Pallas kernels, shards(): pl.pallas_call(hand_over, out_shape=out_shape, in_specs=[whole] * 3, out_...  1.53 us

profile of v2, /device:TPU:1, one launch (start us, length us, event | category | flops | bytes accessed | tf_op | source)
XLA Modules:
  0.0 69.4 jit_solution(8555024247683429211)
XLA Ops:
  0.6 67.2 %shard_map.94 = (bf16[8,4096]{1,0:T(8,128)(2,1)}, f32[8,8]{1,0:T(8,128)}, bf16[8,4096]{1,0:T(8,128)(2,1)}) custom-call(bf16[8,4096]{1,0:T(8,128)(2,1)} %tokens_hbm.1, bf16[8,4096]{1,0:T(8,128)(2,1)} %cotangent_hbm.1, s32[8,8]{1,0:T(8,128)} %ids_hbm.1, f32[8,8]{1,0:T(8,128)} %gates_hbm.1, bf16[1,4096,768]{2,1,0:T(8,128)(2,1)} %gate_hbm.1, ...), custom_call_target="tpu_custom_call" | custom-call | tf_op jit(solution)/shard_map/pallas_call | solution.py:509
  67.8 1.5 %shard_map.95 = (bf16[8,4096]{1,0:T(8,128)(2,1)}, f32[8,8]{1,0:T(8,128)}, bf16[8,4096]{1,0:T(8,128)(2,1)}) custom-call(bf16[8,4096]{1,0:T(8,128)(2,1)} %get-tuple-element.6.refs_0_, f32[8,8]{1,0:T(8,128)} %get-tuple-element.7.refs_1_, bf16[8,4096]{1,0:T(8,128)(2,1)} %get-tuple-element.8.refs_2_), custom_call_target="tpu_custom_call" | custom-call | tf_op jit(solution)/shard_map/pallas_call | solution.py:551

commit v3 on v2

--- a/solution.py
+++ b/solution.py
@@ -169,7 +169,7 @@
         pltpu.make_async_copy(ref, ref, sem).wait()
 
     def ring(axis, source, target, send_sem, recv_sem):
-        for offset in range(1, RING):
+        for offset in (2, 1, 3):
             there = moved(place, axis, (place[axis] + offset) % RING)
             pltpu.make_async_remote_copy(
                 src_ref=source(there[axis]),
@@ -208,8 +208,6 @@
                 first, lambda there: home, lambda offset: home,
                 s1_send.at[kind], s1_recv.at[kind, p],
             )
-    for load in loads:
-        load.start()
     for kind, rows in enumerate(kinds):
         for p in PARTS:
             first, middle, last = ORDERS[p]
@@ -219,6 +217,9 @@
                 middle, lambda there: home, lambda offset: home,
                 s2_send.at[kind], s2_recv.at[kind, p],
             )
+
+    for load in loads:
+        load.start()
 
     r0, r1 = iota((SLOTS, SLOTS), 0), iota((SLOTS, SLOTS), 1)
     same = (r0 // 2) % 16 == r1 // 16

time: 69.6 us -> 68.8 us (0.989)
  Pallas kernels: 68.7 us -> 68 us
    pallas_call x1, Pallas kernels: 67.2 us -> 66.4 us  [shards(): pl.pallas_call(kernel, out_shape=out_shape, in_specs=[hbm] * 7, out_specs...]
where the time goes in v3:
time: 68.8 us; the launch traced here: 68.6 us
  Pallas kernels  68 us (99%)
    pallas_call x1, Pallas kernels, shards(): pl.pallas_call(kernel, out_shape=out_shape, in_specs=[hbm] * 7, out_specs...  66.4 us
    pallas_call x1, Pallas kernels, shards(): pl.pallas_call(hand_over, out_shape=out_shape, in_specs=[whole] * 3, out_...  1.53 us

profile of v3, /device:TPU:1, one launch (start us, length us, event | category | flops | bytes accessed | tf_op | source)
XLA Modules:
  0.0 68.6 jit_solution(6412022606328933075)
XLA Ops:
  0.6 66.4 %shard_map.94 = (bf16[8,4096]{1,0:T(8,128)(2,1)}, f32[8,8]{1,0:T(8,128)}, bf16[8,4096]{1,0:T(8,128)(2,1)}) custom-call(bf16[8,4096]{1,0:T(8,128)(2,1)} %tokens_hbm.1, bf16[8,4096]{1,0:T(8,128)(2,1)} %cotangent_hbm.1, s32[8,8]{1,0:T(8,128)} %ids_hbm.1, f32[8,8]{1,0:T(8,128)} %gates_hbm.1, bf16[1,4096,768]{2,1,0:T(8,128)(2,1)} %gate_hbm.1, ...), custom_call_target="tpu_custom_call" | custom-call | tf_op jit(solution)/shard_map/pallas_call | solution.py:510
  67.1 1.5 %shard_map.95 = (bf16[8,4096]{1,0:T(8,128)(2,1)}, f32[8,8]{1,0:T(8,128)}, bf16[8,4096]{1,0:T(8,128)(2,1)}) custom-call(bf16[8,4096]{1,0:T(8,128)(2,1)} %get-tuple-element.6.refs_0_, f32[8,8]{1,0:T(8,128)} %get-tuple-element.7.refs_1_, bf16[8,4096]{1,0:T(8,128)(2,1)} %get-tuple-element.8.refs_2_), custom_call_target="tpu_custom_call" | custom-call | tf_op jit(solution)/shard_map/pallas_call | solution.py:552

commit v4 on v3

--- a/solution.py
+++ b/solution.py
@@ -218,8 +218,8 @@
                 s2_send.at[kind], s2_recv.at[kind, p],
             )
 
-    for load in loads:
-        load.start()
+    loads[0].start()
+    loads[1].start()
 
     r0, r1 = iota((SLOTS, SLOTS), 0), iota((SLOTS, SLOTS), 1)
     same = (r0 // 2) % 16 == r1 // 16
@@ -278,6 +278,8 @@
         exchange(
             ORDERS[p][2], grad_send.at[p], grad_recv.at[p], c3_send.at[0], c3_recv.at[p]
         )
+
+    loads[2].start()
 
     def in_order(p, rows):
         return rows if p == 0 else dot(reorder(p, True), rows).astype(BF16)

time: 68.8 us -> 68.8 us (level)
  no operation moved by 1% of the time
where the time goes in v4:
time: 68.8 us; the launch traced here: 68.6 us
  Pallas kernels  68 us (99%)
    pallas_call x1, Pallas kernels, shards(): pl.pallas_call(kernel, out_shape=out_shape, in_specs=[hbm] * 7, out_specs...  66.4 us
    pallas_call x1, Pallas kernels, shards(): pl.pallas_call(hand_over, out_shape=out_shape, in_specs=[whole] * 3, out_...  1.53 us

profile of v4, /device:TPU:1, one launch (start us, length us, event | category | flops | bytes accessed | tf_op | source)
XLA Modules:
  0.0 68.6 jit_solution(10530792278447592935)
XLA Ops:
  0.6 66.4 %shard_map.94 = (bf16[8,4096]{1,0:T(8,128)(2,1)}, f32[8,8]{1,0:T(8,128)}, bf16[8,4096]{1,0:T(8,128)(2,1)}) custom-call(bf16[8,4096]{1,0:T(8,128)(2,1)} %tokens_hbm.1, bf16[8,4096]{1,0:T(8,128)(2,1)} %cotangent_hbm.1, s32[8,8]{1,0:T(8,128)} %ids_hbm.1, f32[8,8]{1,0:T(8,128)} %gates_hbm.1, bf16[1,4096,768]{2,1,0:T(8,128)(2,1)} %gate_hbm.1, ...), custom_call_target="tpu_custom_call" | custom-call | tf_op jit(solution)/shard_map/pallas_call | solution.py:512
  67.1 1.5 %shard_map.95 = (bf16[8,4096]{1,0:T(8,128)(2,1)}, f32[8,8]{1,0:T(8,128)}, bf16[8,4096]{1,0:T(8,128)(2,1)}) custom-call(bf16[8,4096]{1,0:T(8,128)(2,1)} %get-tuple-element.6.refs_0_, f32[8,8]{1,0:T(8,128)} %get-tuple-element.7.refs_1_, bf16[8,4096]{1,0:T(8,128)(2,1)} %get-tuple-element.8.refs_2_), custom_call_target="tpu_custom_call" | custom-call | tf_op jit(solution)/shard_map/pallas_call | solution.py:554
